TPU v7x, 32 devices: a whole 2x2x4 slice. The times are simulated.
32 devices in a mesh: box: 8 (over z, y), dir: 4 (over x, core).
Axes of the slice: x: 2, y: 2, z: 4, core: 2. Of those that a mesh axis runs over, the one named last changes fastest.
Arguments:
- pattern: bfloat16 [2, 32, 16, 128, 256], P(None, 'box', None, 'dir'), may hold values from -6 to 6
- occupied: int32 [32, 16], P('box'), may hold values from 0 to 1, as said below
- trans_fine: bfloat16 [2, 40, 128, 256], P(None, None, 'dir'), may hold values from -1.25 to 1.25
- trans_coarse: bfloat16 [2, 40, 256, 512], P(None, None, 'dir'), may hold values from -1.25 to 1.25
- theta_weights: bfloat16 [256, 4], P('dir'), may hold values from -0.19921875 to 0.796875
- phi_matrix: bfloat16 [256, 512], replicated, may hold values from -0.375 to 0.375
- child_phase: float32 [4, 256, 512], P(None, 'dir'), may hold values from -3.140625 to 3.140625
Outputs:
- local_fine: bfloat16 [2, 32, 16, 128, 256], P(None, 'box', None, 'dir')
- local_coarse: bfloat16 [2, 16, 8, 256, 512], P(None, 'box', None, 'dir')
Inputs may be any that keep to these rules, and one draw needn't show every extreme that they name: `occupied`: 1 for a box that holds unknowns, 0 for an empty one.
All inputs are finite; a program needn't handle non-finite values.
Results may differ from a plain program's by a relative error of at most 0.0057.
Values may be sent and summed in bfloat16 or wider, within the bound.
No kernel may reach another device: no remote copies, remote signals or barrier semaphores. Data moves between devices by JAX's collectives and lax.ppermute only.
A program may use at most 320 MiB of HBM per device.

v0:
```python
import jax
import jax.numpy as jnp
from jax import lax
from jax.sharding import PartitionSpec as P

far_offsets = [
    (step_row, step_col)
    for step_row in range(-3, 4)
    for step_col in range(-3, 4)
    if max(abs(step_row), abs(step_col)) >= 2
]


def extended_2(value, sides, width):
    for axis, dim in sides:
        size, length = (lax.axis_size(axis), value.shape[dim])
        up = [(i, (i + 1) % size) for i in range(size - 1)]
        down = [(j, i) for i, j in up]
        last = lax.slice_in_dim(value, length - width, length, axis=dim)
        initial = lax.slice_in_dim(value, 0, width, axis=dim)
        before = lax.ppermute(last, axis, up)
        after = lax.ppermute(initial, axis, down)
        value = jnp.concatenate([before, value, after], axis=dim)
    return value


def allowed(parity, step):
    if step == 3:
        return 1.0 - parity
    if step == -3:
        return parity
    return jnp.ones_like(parity)


def widen(slab):
    return jnp.pad(slab, ((0, 0), (1, 1), (0, 0), (0, 0), (0, 0)))


def translate(extended, table, occupied_dest, first_row):
    count_rows = extended.shape[1] - 6
    count_cols = extended.shape[2]
    padded = jnp.pad(extended, ((0, 0), (0, 0), (3, 3), (0, 0), (0, 0)))
    row_parity = ((first_row + jnp.arange(count_rows, dtype=jnp.int32)) % 2).astype(jnp.float32)
    col_parity = (jnp.arange(count_cols, dtype=jnp.int32) % 2).astype(jnp.float32)
    shape = (count_rows, count_cols, extended.shape[3], extended.shape[4])
    real_sum = jnp.zeros(shape, jnp.float32)
    imag_sum = jnp.zeros(shape, jnp.float32)
    for offset_code, (step_row, step_col) in enumerate(far_offsets):
        weight = allowed(row_parity, step_row)[:, None] * allowed(col_parity, step_col)[None, :]
        weight = weight[:, :, None, None]
        source = padded[
            :, 3 + step_row : 3 + step_row + count_rows, 3 + step_col : 3 + step_col + count_cols
        ].astype(jnp.float32)
        factor_real = table[0, offset_code].astype(jnp.float32)
        factor_imag = table[1, offset_code].astype(jnp.float32)
        real_sum = real_sum + weight * (source[0] * factor_real - source[1] * factor_imag)
        imag_sum = imag_sum + weight * (source[0] * factor_imag + source[1] * factor_real)
    dest = occupied_dest.astype(jnp.float32)[:, :, None, None]
    return jnp.stack([real_sum * dest, imag_sum * dest])


def aggregate(theta_ext, theta_weights, phi_matrix, child_phase):
    theta_rows = theta_weights.shape[0]
    columns = theta_ext.shape[3]
    row_ids = jnp.arange(theta_rows, dtype=jnp.int32)[:, None]
    col_ids = jnp.arange(columns, dtype=jnp.int32)[None, :]
    band = jnp.zeros((theta_rows, columns), jnp.float32)
    for stencil in range(4):
        band = band + jnp.where(
            col_ids == row_ids // 2 + 1 + stencil,
            theta_weights[:, stencil : stencil + 1].astype(jnp.float32),
            0.0,
        )
    band = band.astype(jnp.bfloat16)
    theta_part = jnp.einsum(
        "rc,xijcp->xijrp", band, theta_ext, preferred_element_type=jnp.float32
    ).astype(jnp.bfloat16)
    count_rows, count_cols = (theta_ext.shape[1], theta_ext.shape[2])
    azimuths = phi_matrix.shape[1]
    full = jnp.dot(
        theta_part.reshape(-1, phi_matrix.shape[0]), phi_matrix, preferred_element_type=jnp.float32
    )
    full = full.reshape(2, count_rows // 2, 2, count_cols // 2, 2, theta_rows, azimuths)
    phase_cos = jnp.cos(child_phase).reshape(2, 2, theta_rows, azimuths)[None, :, None, :, :, :]
    phase_sin = jnp.sin(child_phase).reshape(2, 2, theta_rows, azimuths)[None, :, None, :, :, :]
    real_part = jnp.sum(phase_cos * full[0] - phase_sin * full[1], axis=(1, 3))
    imag_part = jnp.sum(phase_cos * full[1] + phase_sin * full[0], axis=(1, 3))
    return jnp.stack([real_part, imag_part]).astype(jnp.bfloat16)


def local(pattern, occupied, trans_fine, trans_coarse, theta_weights, phi_matrix, child_phase):
    count_rows = pattern.shape[1]
    count_cols = pattern.shape[2]
    group = lax.axis_index("box")
    masked = pattern * occupied.astype(jnp.bfloat16)[None, :, :, None, None]
    box_ext = extended_2(masked, (("box", 1),), 2)
    local_fine = translate(widen(box_ext), trans_fine, occupied, group * count_rows).astype(
        jnp.bfloat16
    )
    theta_ext = extended_2(masked, (("dir", 3),), 2)
    coarse = aggregate(theta_ext, theta_weights, phi_matrix, child_phase)
    occupied_coarse = jnp.max(occupied.reshape(count_rows // 2, 2, count_cols // 2, 2), axis=(1, 3))
    coarse_rows = coarse.shape[1]
    extended = extended_2(coarse, (("box", 1),), 2)
    local_coarse = translate(
        widen(extended), trans_coarse, occupied_coarse, group * coarse_rows
    ).astype(jnp.bfloat16)
    return (local_fine, local_coarse)


def solution(mesh):
    return jax.shard_map(
        local,
        mesh=mesh,
        in_specs=(
            P(None, "box", None, "dir", None),
            P("box", None),
            P(None, None, "dir", None),
            P(None, None, "dir", None),
            P("dir", None),
            P(),
            P(None, "dir", None),
        ),
        out_specs=(P(None, "box", None, "dir", None), P(None, "box", None, "dir", None)),
        check_vma=False,
    )
```

profile of v0, /device:TPU:0, one launch (start us, length us, event | category | flops | bytes accessed | tf_op | source)
XLA Modules:
  0.0 469.6 jit_solution(3033490392209774396)
XLA Ops:
  0.6 0.0 copy-start
  0.6 1.4 fusion.112
  2.0 1.8 broadcast_multiply_fusion
  3.8 1.5 fusion.110
  5.3 1.3 collective-permute-start.1
  6.6 6.5 %collective-permute-start = (bf16[2,2,16,32,256]{4,3,2,1,0:T(8,128)(2,1)}, bf16[2,2,16,32,256]{4,3,2,1,0:T(8,128)(2,1)}, u32[]{:S(2)}, u32[]{:S(2)}) collective-permute-start(bf16[2,2,16,32,256]{4,3,2,1,0:T(8,128)(2,1)} %get-tuple-element.166), channel_id=1, source_target_pairs={{0,4},{4,8},{8,12},{12,16},{16,20},{20,24},{24,28},{1,5},{5,9},{9,... | collective-permute-start | bytes 3145736 | tf_op jit(solution)/shard_map/ppermute | solution.py:21
  13.1 0.3 fusion.109
  13.4 1.3 collective-permute-start.3
  14.7 3.7 collective-permute-start.2
  18.4 0.0 copy-start.45
  18.5 1.4 bitcast_convert_fusion.155
  19.9 1.7 bitcast_convert_fusion.159
  21.7 1.8 bitcast_convert_fusion.158
  23.4 1.8 bitcast_convert_fusion.157
  25.2 1.8 bitcast_convert_fusion.156
  27.1 0.0 copy-start.41
  27.1 1.7 bitcast_convert_fusion.75
  28.8 2.8 bitcast_convert_fusion.79
  31.6 2.7 bitcast_convert_fusion.78
  34.3 2.7 bitcast_convert_fusion.77
  37.1 0.0 copy-start.47
  37.1 0.0 copy-start.20
  37.1 0.0 copy-start.34
  37.1 2.9 bitcast_convert_fusion.76
  40.0 2.6 fusion.111
  42.6 0.0 copy-done.44
  42.6 0.6 broadcast_multiply_fusion.4
  43.2 0.0 copy-done.37
  43.3 0.7 broadcast_multiply_fusion.8
  43.9 0.1 reshape.351
  44.0 0.1 reduce_max.9
  44.1 0.5 convert_element_type.818
  44.7 0.0 collective-permute-done.3
  44.7 0.0 collective-permute-done.2
  44.7 2.3 convolution_convert_fusion
  47.0 2.3 fusion.113
  49.3 0.0 copy-start.8
  49.3 6.7 %fusion.108 = (f32[4096,512]{1,0:T(8,128)}, f32[4096,512]{1,0:T(8,128)}) fusion(f32[8192,512]{1,0:T(8,128)S(1)} %fusion.113), kind=kLoop, calls=%fused_computation.401 | loop fusion | bytes 33554432 | tf_op jit(solution)/shard_map/slice | solution.py:86
  56.0 7.7 %subtract_reduce_fusion = (bf16[2,8,64,512]{3,2,1,0:T(8,128)(2,1)S(1)}, bf16[2,8,64,512]{3,2,1,0:T(8,128)(2,1)S(1)}) fusion(f32[2,2,8,2,64,512]{5,4,3,2,1,0:T(8,128)} %bitcast.513, f32[2,2,8,2,64,512]{5,4,3,2,1,0:T(8,128)} %bitcast.512, f32[2,2,64,512]{3,2,1,0:T(8,128)S(1)} %bitcast.520, f32[2,2,64,512]{3,2,1,0:T(8,128)S(1)} %bitcast.519), kind=kLoop, calls=%fused_computation.84 | loop fusion | flops 15728640 | bytes 19922944 | tf_op jit(solution)/shard_map/reduce_sum | solution.py:86
  63.8 1.7 pad_maximum_fusion.3
  65.5 0.4 copy-done.6
  65.8 1.3 collective-permute-start.5
  67.1 6.1 %collective-permute-start.4 = (bf16[2,2,8,64,512]{4,3,2,1,0:T(8,128)(2,1)}, bf16[2,2,8,64,512]{4,3,2,1,0:T(8,128)(2,1)}, u32[]{:S(2)}, u32[]{:S(2)}) collective-permute-start(bf16[2,2,8,64,512]{4,3,2,1,0:T(8,128)(2,1)} %pad_maximum_fusion.3), channel_id=1, source_target_pairs={{0,4},{4,8},{8,12},{12,16},{16,20},{20,24},{24,28},{1,5},{5,9},{9,... | collective-permute-start | bytes 6291464 | tf_op jit(solution)/shard_map/ppermute | solution.py:21
  73.2 0.0 collective-permute-done.1
  73.2 0.0 collective-permute-done
  73.2 4.6 fusion.9
  77.8 35.7 %slice_convert_fusion.3 = (f32[2,4,16,32,256]{4,3,2,1,0:T(8,128)}, f32[2,4,16,32,256]{4,3,2,1,0:T(8,128)}, f32[2,4,16,32,256]{4,3,2,1,0:T(8,128)}, f32[2,4,16,32...) fusion(bf16[2,10,16,32,256]{4,3,2,1,0:T(8,128)(2,1)} %fusion.9), kind=kLoop, calls=%fused_computation.175 | loop fusion | flops 19922944 | bytes 89128960 | tf_op jit(solution)/shard_map/convert_element_type | solution.py:53
  113.5 35.4 %fusion.15 = (f32[2,4,16,32,256]{4,3,2,1,0:T(8,128)}, f32[2,4,16,32,256]{4,3,2,1,0:T(8,128)}, f32[2,4,16,32,256]{4,3,2,1,0:T(8,128)}, f32[2,4,16,32,256]{4,3,2,1...) fusion(bf16[2,10,16,32,256]{4,3,2,1,0:T(8,128)(2,1)} %fusion.9), kind=kLoop, calls=%fused_computation.96 | loop fusion | flops 19922944 | bytes 84934656 | tf_op jit(solution)/shard_map/convert_element_type | solution.py:53
  149.0 5.6 %fusion.88 = (f32[2,4,16,32,256]{4,3,2,1,0:T(8,128)}, f32[2,4,16,32,256]{4,3,2,1,0:T(8,128)}) fusion(bf16[2,4,16,32,256]{4,3,2,1,0:T(8,128)(2,1)S(1)} %broadcast_multiply_fusion, bf16[2,2,16,32,256]{4,3,2,1,0:T(8,128)(2,1)} %collective-permute-done, bf16[2,2,16,32,256]{4,3,2,1,0:T(8,128)(2,1)} %collective-permute-done.1), kind=kLoop, calls=%fused_computation.174 | loop fusion | flops 4194304 | bytes 12582912 | tf_op jit(solution)/shard_map/convert_element_type | solution.py:53
  154.6 53.4 %multiply_convert_fusion.2 = bf16[1,4,16,32,256]{4,3,2,1,0:T(8,128)(2,1)S(1)} fusion(f32[2,4,16,32,256]{4,3,2,1,0:T(8,128)} %get-tuple-element.160, f32[2,4,16,32,256]{4,3,2,1,0:T(8,128)} %get-tuple-element.159, f32[2,4,16,32,256]{4,3,2,1,0:T(8,128)} %get-tuple-element.158, f32[2,4,16,32,256]{4,3,2,1,0:T(8,128)} %get-tuple-element.161, ...), kind=kLoop, calls=%fused_computation.181 | loop fusion | flops 96993280 | bytes 171443616 | tf_op jit(solution)/shard_map/convert.171
  208.1 53.7 %multiply_convert_fusion.3 = bf16[1,4,16,32,256]{4,3,2,1,0:T(8,128)(2,1)S(1)} fusion(f32[2,4,16,32,256]{4,3,2,1,0:T(8,128)} %get-tuple-element.160, f32[2,4,16,32,256]{4,3,2,1,0:T(8,128)} %get-tuple-element.159, f32[2,4,16,32,256]{4,3,2,1,0:T(8,128)} %get-tuple-element.158, f32[2,4,16,32,256]{4,3,2,1,0:T(8,128)} %get-tuple-element.161, ...), kind=kLoop, calls=%fused_computation.182 | loop fusion | flops 96993280 | bytes 171443616 | tf_op jit(solution)/shard_map/convert.170
  261.8 1.5 pad_maximum_fusion.2
  263.3 0.0 collective-permute-done.5
  263.3 0.0 collective-permute-done.4
  263.3 0.8 copy-done.7
  264.1 6.0 %select_maximum_fusion = bf16[2,8,8,64,512]{4,3,2,1,0:T(8,128)(2,1)} fusion(bf16[2,2,8,64,512]{4,3,2,1,0:T(8,128)(2,1)} %collective-permute-done.5, bf16[2,2,8,64,512]{4,3,2,1,0:T(8,128)(2,1)} %collective-permute-done.4, bf16[1,2,8,64,512]{4,3,2,1,0:T(8,128)(2,1)S(1)} %bitcast.517, bf16[1,2,8,64,512]{4,3,2,1,0:T(8,128)(2,1)S(1)} %bitcast.515), kind=kLoop, calls=%fused_computation.78 | loop fusion | flops 62914560 | bytes 14680064 | tf_op jit(solution)/shard_map/concatenate | solution.py:23
  270.1 35.0 %slice_convert_fusion.1 = (f32[2,2,8,64,512]{4,3,2,1,0:T(8,128)}, f32[2,2,8,64,512]{4,3,2,1,0:T(8,128)}, f32[2,2,8,64,512]{4,3,2,1,0:T(8,128)}, f32[2,2,8,64,512...) fusion(bf16[2,8,8,64,512]{4,3,2,1,0:T(8,128)(2,1)} %select_maxi, ...), kind=kLoop, calls=%fused_computation.169 | loop fusion | flops 19922944 | bytes 92274688 | tf_op jit(solution)/shard_map/convert_element_type | solution.py:53
  305.2 34.9 %fusion.51 = (f32[2,2,8,64,512]{4,3,2,1,0:T(8,128)}, f32[2,2,8,64,512]{4,3,2,1,0:T(8,128)}, f32[2,2,8,64,512]{4,3,2,1,0:T(8,128)}, f32[2,2,8,64,512]{4,3,2,1,0:T...) fusion(bf16[2,8,8,64,512]{4,3,2,1,0:T(8,128)(2,1)} %select_maxi, ...), kind=kLoop, calls=%fused_computation.132 | loop fusion | flops 19922944 | bytes 88080384 | tf_op jit(solution)/shard_map/convert_element_type | solution.py:53
  340.1 4.1 convert_element_type.807
  344.4 4.3 convert_element_type.788
  348.9 59.0 %multiply_convert_fusion = bf16[1,2,8,64,512]{4,3,2,1,0:T(8,128)(2,1)S(1)} fusion(f32[2,2,8,64,512]{4,3,2,1,0:T(8,128)} %get-tuple-element.42, f32[2,2,8,64,512]{4,3,2,1,0:T(8,128)} %get-tuple-element.41, f32[2,2,8,64,512]{4,3,2,1,0:T(8,128)} %get-tuple-element.40, f32[2,2,8,64,512]{4,3,2,1,0:T(8,128)} %get-tuple-element.43, ...), kind=kLoop, calls=%fused_computation.179 | loop fusion | flops 96993280 | bytes 179306896 | tf_op jit(solution)/shard_map/convert.165
  408.0 0.0 copy-start.1
  408.0 59.6 %multiply_convert_fusion.1 = bf16[1,2,8,64,512]{4,3,2,1,0:T(8,128)(2,1)S(1)} fusion(f32[2,2,8,64,512]{4,3,2,1,0:T(8,128)} %get-tuple-element.42, f32[2,2,8,64,512]{4,3,2,1,0:T(8,128)} %get-tuple-element.41, f32[2,2,8,64,512]{4,3,2,1,0:T(8,128)} %get-tuple-element.40, f32[2,2,8,64,512]{4,3,2,1,0:T(8,128)} %get-tuple-element.43, ...), kind=kLoop, calls=%fused_computation.180 | loop fusion | flops 96993280 | bytes 179306896 | tf_op jit(solution)/shard_map/convert.164
  467.6 1.5 pad_maximum_fusion.4
  (95 shorter events, 0.3 us)
Async XLA Ops:
  0.6 46.3 %copy-start = (bf16[256,512]{1,0:T(8,128)(2,1)S(1)}, bf16[256,512]{1,0:T(8,128)(2,1)}, u32[]{:S(2)}) copy-start(bf16[256,512]{1,0:T(8,128)(2,1)} %param.12) | copy-start | bytes 786436
  5.3 67.9 %collective-permute-start.1 = (bf16[2,2,16,32,256]{4,3,2,1,0:T(8,128)(2,1)}, bf16[2,2,16,32,256]{4,3,2,1,0:T(8,128)(2,1)}, u32[]{:S(2)}, u32[]{:S(2)}) collective-permute-start(bf16[2,2,16,32,256]{4,3,2,1,0:T(8,128)(2,1)} %get-tuple-element.167), channel_id=1, source_target_pairs={{4,0},{8,4},{12,8},{16,12},{20,16},{24,20},{28,24},{5,1},{9,5},{13... | collective-permute-start | bytes 3145736 | tf_op jit(solution)/shard_map/ppermute | solution.py:22
  6.6 66.6 %collective-permute-start = (bf16[2,2,16,32,256]{4,3,2,1,0:T(8,128)(2,1)}, bf16[2,2,16,32,256]{4,3,2,1,0:T(8,128)(2,1)}, u32[]{:S(2)}, u32[]{:S(2)}) collective-permute-start(bf16[2,2,16,32,256]{4,3,2,1,0:T(8,128)(2,1)} %get-tuple-element.166), channel_id=1, source_target_pairs={{0,4},{4,8},{8,12},{12,16},{16,20},{20,24},{24,28},{1,5},{5,9},{9,... | collective-permute-start | bytes 3145736 | tf_op jit(solution)/shard_map/ppermute | solution.py:21
  13.4 31.3 %collective-permute-start.3 = (bf16[2,4,16,2,256]{4,3,2,1,0:T(2,128)(2,1)S(1)}, bf16[2,4,16,2,256]{4,3,2,1,0:T(2,128)(2,1)S(1)}, u32[]{:S(2)}, u32[]{:S(2)}) collective-permute-start(bf16[2,4,16,2,256]{4,3,2,1,0:T(2,128)(2,1)S(1)} %get-tuple-element.163), channel_id=1, source_target_pairs={{1,0},{2,1},{3,2},{5,4},{6,5},{7,6},{9,8},{10,9},{11,10},{13,12},{... | collective-permute-start | bytes 393224 | tf_op jit(solution)/shard_map/ppermute | solution.py:22
  14.7 30.0 %collective-permute-start.2 = (bf16[2,4,16,2,256]{4,3,2,1,0:T(2,128)(2,1)S(1)}, bf16[2,4,16,2,256]{4,3,2,1,0:T(2,128)(2,1)}, u32[]{:S(2)}, u32[]{:S(2)}) collective-permute-start(bf16[2,4,16,2,256]{4,3,2,1,0:T(2,128)(2,1)S(1)} %get-tuple-element.162), channel_id=1, source_target_pairs={{0,1},{1,2},{2,3},{4,5},{5,6},{6,7},{8,9},{9,10},{10,11},{12,13},{... | collective-permute-start | bytes 393224 | tf_op jit(solution)/shard_map/ppermute | solution.py:21
  18.4 24.2 %copy-start.43 = (f32[16]{0:T(128)}, f32[16]{0:T(128)S(1)}, u32[]{:S(2)}) copy-start(f32[16]{0:T(128)S(1)} %fusion.101) | copy-start | bytes 196
  18.4 24.2 %copy-start.44 = (f32[16]{0:T(128)}, f32[16]{0:T(128)S(1)}, u32[]{:S(2)}) copy-start(f32[16]{0:T(128)S(1)} %broadcast_subtract_fusion.3) | copy-start | bytes 196
  18.4 24.2 %copy-start.45 = (f32[4]{0:T(128)}, f32[4]{0:T(128)S(1)}, u32[]{:S(2)}) copy-start(f32[4]{0:T(128)S(1)} %fusion.100) | copy-start | bytes 52
  18.5 24.1 %copy-start.46 = (f32[4]{0:T(128)}, f32[4]{0:T(128)S(1)}, u32[]{:S(2)}) copy-start(f32[4]{0:T(128)S(1)} %broadcast_subtract_fusion.2) | copy-start | bytes 52
  27.0 16.3 %copy-start.35 = (f32[8]{0:T(128)}, f32[8]{0:T(128)S(1)}, u32[]{:S(2)}) copy-start(f32[8]{0:T(128)S(1)} %fusion.103) | copy-start | bytes 100
  27.0 16.2 %copy-start.37 = (f32[8]{0:T(128)}, f32[8]{0:T(128)S(1)}, u32[]{:S(2)}) copy-start(f32[8]{0:T(128)S(1)} %broadcast_subtract_fusion.1) | copy-start | bytes 100
  27.0 16.2 %copy-start.39 = (f32[2]{0:T(128)}, f32[2]{0:T(128)S(1)}, u32[]{:S(2)}) copy-start(f32[2]{0:T(128)S(1)} %fusion.102) | copy-start | bytes 28
  27.1 16.2 %copy-start.41 = (f32[2]{0:T(128)}, f32[2]{0:T(128)S(1)}, u32[]{:S(2)}) copy-start(f32[2]{0:T(128)S(1)} %broadcast_subtract_fusion) | copy-start | bytes 28
  37.1 2.9 copy-start.47
  37.1 2.9 copy-start.20
  37.1 6.8 %copy-start.34 = (s32[4,16]{1,0:T(4,128)S(1)}, s32[4,16]{1,0:T(4,128)}, u32[]{:S(2)}) copy-start(s32[4,16]{1,0:T(4,128)} %param.8) | copy-start | bytes 772
  49.3 6.8 %copy-start.8 = (f32[4,64,512]{2,1,0:T(8,128)S(1)}, f32[4,64,512]{2,1,0:T(8,128)}, u32[]{:S(2)}) copy-start(f32[4,64,512]{2,1,0:T(8,128)} %get-tuple-element.249) | copy-start | bytes 1572868
  63.7 1.7 copy-start.4
  63.7 2.1 copy-start.6
  65.8 197.5 %collective-permute-start.5 = (bf16[2,2,8,64,512]{4,3,2,1,0:T(8,128)(2,1)}, bf16[2,2,8,64,512]{4,3,2,1,0:T(8,128)(2,1)}, u32[]{:S(2)}, u32[]{:S(2)}) collective-permute-start(bf16[2,2,8,64,512]{4,3,2,1,0:T(8,128)(2,1)} %pad_maximum_fusion.3), channel_id=1, source_target_pairs={{4,0},{8,4},{12,8},{16,12},{20,16},{24,20},{28,24},{5,1},{9,5},{13... | collective-permute-start | bytes 6291464 | tf_op jit(solution)/shard_map/ppermute | solution.py:22
  67.1 196.2 %collective-permute-start.4 = (bf16[2,2,8,64,512]{4,3,2,1,0:T(8,128)(2,1)}, bf16[2,2,8,64,512]{4,3,2,1,0:T(8,128)(2,1)}, u32[]{:S(2)}, u32[]{:S(2)}) collective-permute-start(bf16[2,2,8,64,512]{4,3,2,1,0:T(8,128)(2,1)} %pad_maximum_fusion.3), channel_id=1, source_target_pairs={{0,4},{4,8},{8,12},{12,16},{16,20},{20,24},{24,28},{1,5},{5,9},{9,... | collective-permute-start | bytes 6291464 | tf_op jit(solution)/shard_map/ppermute | solution.py:21
  148.9 5.6 %copy-start.2 = (f32[2,4,16,32,256]{4,3,2,1,0:T(8,128)S(1)}, f32[2,4,16,32,256]{4,3,2,1,0:T(8,128)}, u32[]{:S(2)}) copy-start(f32[2,4,16,32,256]{4,3,2,1,0:T(8,128)} %get-tuple-element.143) | copy-start | bytes 12582916
  148.9 5.6 %copy-start.21 = (f32[32,256]{1,0:T(8,128)S(1)}, f32[32,256]{1,0:T(8,128)}, u32[]{:S(2)}) copy-start(f32[32,256]{1,0:T(8,128)} %get-tuple-element.173) | copy-start | bytes 98308
  148.9 5.6 %copy-start.22 = (f32[32,256]{1,0:T(8,128)S(1)}, f32[32,256]{1,0:T(8,128)}, u32[]{:S(2)}) copy-start(f32[32,256]{1,0:T(8,128)} %get-tuple-element.174) | copy-start | bytes 98308
  149.0 5.6 %copy-start.23 = (f32[32,256]{1,0:T(8,128)S(1)}, f32[32,256]{1,0:T(8,128)}, u32[]{:S(2)}) copy-start(f32[32,256]{1,0:T(8,128)} %get-tuple-element.175) | copy-start | bytes 98308
  149.0 5.6 %copy-start.24 = (f32[32,256]{1,0:T(8,128)S(1)}, f32[32,256]{1,0:T(8,128)}, u32[]{:S(2)}) copy-start(f32[32,256]{1,0:T(8,128)} %get-tuple-element.176) | copy-start | bytes 98308
  149.0 5.6 %copy-start.25 = (f32[32,256]{1,0:T(8,128)S(1)}, f32[32,256]{1,0:T(8,128)}, u32[]{:S(2)}) copy-start(f32[32,256]{1,0:T(8,128)} %get-tuple-element.177) | copy-start | bytes 98308
  149.0 5.6 %copy-start.26 = (f32[32,256]{1,0:T(8,128)S(1)}, f32[32,256]{1,0:T(8,128)}, u32[]{:S(2)}) copy-start(f32[32,256]{1,0:T(8,128)} %get-tuple-element.178) | copy-start | bytes 98308
  149.0 5.6 %copy-start.27 = (f32[32,256]{1,0:T(8,128)S(1)}, f32[32,256]{1,0:T(8,128)}, u32[]{:S(2)}) copy-start(f32[32,256]{1,0:T(8,128)} %get-tuple-element.179) | copy-start | bytes 98308
  149.0 5.6 %copy-start.28 = (f32[32,256]{1,0:T(8,128)S(1)}, f32[32,256]{1,0:T(8,128)}, u32[]{:S(2)}) copy-start(f32[32,256]{1,0:T(8,128)} %get-tuple-element.180) | copy-start | bytes 98308
  261.8 1.5 copy-start.5
  261.8 2.3 copy-start.7
  344.3 4.5 copy-start.3
  344.3 4.5 copy-start.9
  344.3 4.5 copy-start.10
  344.3 4.5 copy-start.11
  344.3 4.5 copy-start.12
  344.3 4.5 copy-start.13
  344.3 4.5 copy-start.14
  344.3 4.5 copy-start.15
  344.3 4.5 copy-start.16
  344.3 4.5 copy-start.17
  344.3 4.5 copy-start.18
  344.3 4.5 copy-start.19
  344.3 4.5 copy-start.29
  344.4 4.5 copy-start.30
  344.4 4.5 copy-start.31
  344.4 4.5 copy-start.32
  344.4 4.5 copy-start.33
  344.4 4.5 copy-start.36
  344.4 4.5 copy-start.38
  344.4 4.5 copy-start.40
  344.4 4.5 copy-start.42
  408.0 61.2 %copy-start.1 = (bf16[256,512]{1,0:T(8,128)(2,1)S(1)}, bf16[256,512]{1,0:T(8,128)(2,1)}, u32[]{:S(2)}) copy-start(bf16[256,512]{1,0:T(8,128)(2,1)} %param.12) | copy-start | bytes 786436
where the time goes:
time: 478 us; the launch traced here: 470 us
  other arithmetic  430 us (90%)
  starting transfers between devices  20.1 us (4%)
  local copies, waits for them, and re-layouts  12.5 us (3%)
    another operation x4, other arithmetic  226 us
    convert_element_type x7, other arithmetic, translate(): source = padded[:, 3 + step_row:3 + step_row + count_rows, 3 + step_col:3...  155 us
    ppermute x3, starting transfers between devices, extended_2(): before = lax.ppermute(last, axis, up)  16.3 us
    mul x6, other arithmetic, translate(): source[0] * factor_real - source[1] * factor_imag  12.2 us
    concatenate x2, other arithmetic, extended_2(): value = jnp.concatenate([before, value, after], axis=dim)  10.7 us
  transfers between devices with their start and end apart: 6, of which 0 were waited for; matrix products, arithmetic and copies ran while one was open for 50% of the time, Pallas kernels for 0%

commit v1 on v0

v1 whole, which is shorter than its diff:
```python
import functools

import jax
import jax.numpy as jnp
from jax import lax
from jax.experimental import pallas as pl
from jax.experimental.pallas import tpu as pltpu
from jax.sharding import PartitionSpec as P

far_offsets = [
    (step_row, step_col)
    for step_row in range(-3, 4)
    for step_col in range(-3, 4)
    if max(abs(step_row), abs(step_col)) >= 2
]
code_of = {step: code for code, step in enumerate(far_offsets)}
LANES = 128
VMEM_BYTES = 48 * 2**20


def steps_of(parity):
    return range(-3, 3) if parity else range(-2, 4)


def halo(masked):
    size = lax.axis_size("dir")
    up = [(i, i + 1) for i in range(size - 1)]
    down = [(j, i) for i, j in up]
    before = lax.ppermute(masked[:, :, :, -2:], "dir", up)
    after = lax.ppermute(masked[:, :, :, :2], "dir", down)
    return jnp.concatenate([before, after], axis=3)


def bands(theta_weights, rows, group):
    theta_rows = theta_weights.shape[0]
    row_ids = jnp.arange(theta_rows, dtype=jnp.int32)[:, None]
    col_ids = jnp.arange(rows + 4, dtype=jnp.int32)[None, :]
    band = jnp.zeros((theta_rows, rows + 4), jnp.float32)
    for stencil in range(4):
        band = band + jnp.where(
            col_ids == row_ids // 2 + 1 + stencil,
            theta_weights[:, stencil : stencil + 1].astype(jnp.float32),
            0.0,
        )
    band = band.astype(jnp.bfloat16)
    inner = band[:, 2 : rows + 2]
    outer = jnp.concatenate([band[:, :2], band[:, rows + 2 :]], axis=1)
    outer = jnp.stack(
        [jnp.pad(outer, ((0, 0), (4 * c, 4 * (group - 1 - c)))) for c in range(group)]
    )
    return inner, outer


def cost(us):
    return pl.CostEstimate(flops=0, bytes_accessed=int(us * 3.3e5), transcendentals=0)


def aggregate_kernel(masked, group, pieces, *refs):
    refs = list(refs)
    flag_ref = refs.pop(0) if masked else None
    m_refs = [refs.pop(0) for _ in range(pieces)]
    h_ref, inner_ref, outer_ref, phi_ref, cos_ref, sin_ref, out_ref, part_ref, full_ref = refs
    theta_rows, polar = inner_ref.shape
    boxes = out_ref.shape[2]
    span = 2 * boxes // pieces
    azimuths, fine = phi_ref.shape
    f32, bf16 = jnp.float32, jnp.bfloat16
    pairs = [(x, a) for x in range(2) for a in range(2)]
    for col in range(2 * boxes):
        blocks = [m_refs[col // span][x, a, col % span] for x, a in pairs]
        if masked:
            row, at = 2 * pl.program_id(0), 2 * boxes * pl.program_id(1) + col
            flags = [flag_ref[row + a, at].astype(f32).astype(bf16) for x, a in pairs]
            blocks = [block * flag for block, flag in zip(blocks, flags)]
        own = jnp.concatenate(blocks, axis=1)
        rows = pl.ds(col // group * 4 * group, 4 * group)
        beside = jnp.concatenate([h_ref[x, a, rows] for x, a in pairs], axis=1)
        outer = outer_ref[col % group]
        if polar % 16 == 0:
            both = jnp.concatenate([inner_ref[...], outer], axis=1)
            part = jnp.dot(both, jnp.concatenate([own, beside], axis=0), preferred_element_type=f32)
        else:
            part = jnp.dot(inner_ref[...], own, preferred_element_type=f32)
            part = part + jnp.dot(outer, beside, preferred_element_type=f32)
        part = part.astype(bf16)
        for n, (x, a) in enumerate(pairs):
            slot = ((col // 2) * 4 + 2 * a + col % 2) * 2 + x
            part_ref[pl.ds(slot * theta_rows, theta_rows), :] = part[:, n * azimuths : (n + 1) * azimuths]
    full = jnp.dot(part_ref[...], phi_ref[...], preferred_element_type=f32)
    full_ref[...] = full.reshape(full_ref.shape)
    tiles = fine // LANES

    def combine(index, carry):
        start = pl.multiple_of((index // tiles) * 16, 16)
        subs = pl.ds(start, 16)
        lanes = pl.ds(pl.multiple_of((index % tiles) * LANES, LANES), LANES)
        phases = [(cos_ref[k, subs, lanes], sin_ref[k, subs, lanes]) for k in range(4)]
        for box in range(boxes):
            real_sum = None
            for k, (phase_cos, phase_sin) in enumerate(phases):
                real, imag = [full_ref[8 * box + 2 * k + x, subs, lanes] for x in range(2)]
                terms = (phase_cos * real - phase_sin * imag, phase_cos * imag + phase_sin * real)
                if real_sum is None:
                    real_sum, imag_sum = terms
                else:
                    real_sum, imag_sum = real_sum + terms[0], imag_sum + terms[1]
            out_ref[0, 0, box, subs, lanes] = real_sum.astype(bf16)
            out_ref[1, 0, box, subs, lanes] = imag_sum.astype(bf16)
        return carry

    lax.fori_loop(0, (theta_rows // 16) * tiles, combine, 0)


def aggregate(held, cols, halos, index, inner, outer, phi_matrix, phase_cos, phase_sin, flags=None):
    _, rows, _, polar, azimuths = held[0].shape
    theta_rows, fine = inner.shape[0], phi_matrix.shape[1]
    group = outer.shape[0]
    pieces = len(held)
    total = cols * pieces
    masked = flags is not None
    return pl.pallas_call(
        functools.partial(aggregate_kernel, masked, group, pieces),
        grid=(rows // 2, 1),
        in_specs=[pl.BlockSpec(memory_space=pltpu.SMEM)] * masked
        + [pl.BlockSpec((2, 2, cols, polar, azimuths), lambda i, j: (0, i, 0, 0, 0))] * pieces
        + [
            pl.BlockSpec((2, 2, 4 * total, azimuths), lambda i, j: (0, i, index, 0)),
            pl.BlockSpec((theta_rows, polar), lambda i, j: (0, 0)),
            pl.BlockSpec((group, theta_rows, 4 * group), lambda i, j: (0, 0, 0)),
            pl.BlockSpec((azimuths, fine), lambda i, j: (0, 0)),
            pl.BlockSpec((4, theta_rows, fine), lambda i, j: (0, 0, 0)),
            pl.BlockSpec((4, theta_rows, fine), lambda i, j: (0, 0, 0)),
        ],
        out_specs=pl.BlockSpec((2, 1, total // 2, theta_rows, fine), lambda i, j: (0, i, 0, 0, 0)),
        out_shape=jax.ShapeDtypeStruct((2, rows // 2, total // 2, theta_rows, fine), jnp.bfloat16),
        scratch_shapes=[
            pltpu.VMEM((4 * total * theta_rows, azimuths), jnp.bfloat16),
            pltpu.VMEM((4 * total, theta_rows, fine), jnp.float32),
        ],
        compiler_params=pltpu.CompilerParams(vmem_limit_bytes=VMEM_BYTES),
        cost_estimate=cost(0.5 * rows * total / 4 + 1),
    )(*[flags] * masked, *held, halos, inner, outer, phi_matrix, phase_cos, phase_sin)


def runs_of(row, rows, own, sides):
    steps = [
        step
        for step in steps_of(row % 2)
        if (own if 0 <= row + step < rows else sides)
    ]
    runs = []
    for step in steps:
        kind = (abs(step) >= 2, step > 0 and abs(step) >= 2)
        if runs and runs[-1][0] == kind and runs[-1][2] == step:
            runs[-1][2] = step + 1
        else:
            runs.append([kind, step, step + 1])
    return [(kind[0], start, stop) for kind, start, stop in runs]


def translate_kernel(plan, odd_ref, dest_ref, *refs):
    own_pieces, swap_pieces, far_pieces, first, last, columns, rows, partial, final, whole = plan
    refs = list(refs)
    own_refs = [refs.pop(0) for _ in own_pieces]
    swap_refs = [refs.pop(0) for _ in swap_pieces]
    far_refs = [refs.pop(0) for _ in far_pieces]
    table_ref = refs.pop(0)
    partial_ref = refs.pop(0) if partial else None
    if whole:
        refs.pop(0)
    out_ref = refs.pop(0)
    source_ref, factor_ref = refs.pop(0), refs.pop(0)
    sum_ref = refs.pop(0) if final else None
    polar, azimuths = table_ref.shape[2], table_ref.shape[3]
    half = min(8, polar)
    even = odd_ref[0] == 0
    wide = last - first
    span = wide + 4
    f32 = jnp.float32
    at_once = 8 if wide % 8 == 0 else wide

    zero = jnp.zeros((polar, LANES), f32)

    def clear(row, carry):
        for col in range(span):
            if not 0 <= first - 2 + col < columns:
                for form in range(3):
                    source_ref[form, row, col] = zero
        return carry

    lax.fori_loop(0, rows + 4, clear, 0)

    def keep(row, col, real, imag, flag=None):
        real, imag = real.astype(f32), imag.astype(f32)
        if flag is not None:
            real, imag = real * flag, imag * flag
        source_ref[0, row, col] = real
        source_ref[1, row, col] = imag
        source_ref[2, row, col] = real + imag

    def tile(index, carry):
        lanes = pl.ds(pl.multiple_of(index * LANES, LANES), LANES)

        def keep_own(row, carry):
            for piece, (start, stop, raw) in enumerate(own_pieces):
                for col in range(max(start, first - 2), min(stop, last + 2)):
                    flag = dest_ref[row, col].astype(f32) if raw else None
                    keep(row + 2, col - (first - 2), *[own_refs[piece][x, row, col - start, :, lanes] for x in range(2)], flag)
            return carry

        def keep_sides(row, carry):
            def load(pieces, piece_refs, col):
                ref, at = [
                    (ref, col - start) for ref, (start, stop) in zip(piece_refs, pieces) if start <= col < stop
                ][0]
                return [ref[x, row, at, :, lanes] for x in range(2)]

            for col in range(max(0, first - 2), min(columns, last + 2)):
                swap, far = load(swap_pieces, swap_refs, col), load(far_pieces, far_refs, col)
                to = col - (first - 2)
                keep(row, to, *[jnp.where(even, far[x], swap[x]) for x in range(2)])
                keep(rows + 2 + row, to, *[jnp.where(even, swap[x], far[x]) for x in range(2)])
            return carry

        if own_pieces:
            lax.fori_loop(0, rows, keep_own, 0)
        if swap_pieces:
            lax.fori_loop(0, 2, keep_sides, 0)

        def keep_factors(block, carry):
            for code in [block * 4 + n for n in range(4)]:
                real = table_ref[0, code, :, lanes].astype(f32)
                imag = table_ref[1, code, :, lanes].astype(f32)
                factor_ref[0, code] = real
                factor_ref[1, code] = imag - real
                factor_ref[2, code] = imag + real
            return carry

        lax.fori_loop(0, len(far_offsets) // 4, keep_factors, 0)

        def part(index, carry):
            subs = pl.ds(pl.multiple_of((index % (polar // half)) * half, half), half)
            begin = (index // (polar // half)) * at_once
            for row in range(rows):

                def one_step(far_row, base, start, row=row):
                    cols = [q for q in range(-3, 4) if far_row or abs(q) >= 2]

                    def body(step, sums):
                        sums = [list(s) for s in sums]
                        found = {}
                        code = base + step * len(cols)
                        for n, step_col in enumerate(cols):
                            factor = [factor_ref[form, code + n, subs] for form in range(3)]
                            for dest in range(at_once):
                                if step_col not in steps_of(dest % 2):
                                    continue
                                col = dest + 2 + step_col
                                if col not in found:
                                    found[col] = [
                                        source_ref[form, row + 2 + start + step, begin + col, subs]
                                        for form in range(3)
                                    ]
                                real, imag, both = found[col]
                                terms = (both * factor[0], real * factor[1], imag * factor[2])
                                sums[dest] = [s + t for s, t in zip(sums[dest], terms)]
                        return tuple(tuple(s) for s in sums)

                    return body

                nothing = jnp.zeros((half, LANES), f32)
                sums = tuple((nothing,) * 3 for _ in range(at_once))
                for far_row, start, stop in runs_of(row, rows, bool(own_pieces), bool(swap_pieces)):
                    base = code_of[start, -3]
                    sums = lax.fori_loop(0, stop - start, one_step(far_row, base, start), sums)
                for dest in range(at_once):
                    shared, cross, other = sums[dest]
                    pair = [shared - other, shared + cross]
                    for x in range(2):
                        value = pair[x]
                        if partial:
                            value = value + partial_ref[x, row, begin + dest, subs, lanes]
                        if final:
                            flag = dest_ref[row, first + begin + dest].astype(f32)
                            sum_ref[x, row, begin + dest, subs] = value * flag
                        else:
                            out_ref[x, row, begin + dest, subs, lanes] = value
            return carry

        lax.fori_loop(0, (polar // half) * (wide // at_once), part, 0)

        def finish(row, carry):
            for x in range(2):
                for dest in range(wide):
                    out_ref[x, row, dest, :, lanes] = sum_ref[x, row, dest].astype(jnp.bfloat16)
            return carry

        if final:
            lax.fori_loop(0, rows, finish, 0)
        return carry

    lax.fori_loop(0, azimuths // LANES, tile, 0)


def translate(own, sides, table, dest, odd, first, last, partial=None, final=True, whole=None, raw=False, part=(0, 1)):
    rows, columns = dest.shape
    polar, azimuths = table.shape[2], table.shape[3]
    block = min(16, polar)
    edge = rows // 2 - 1
    wide = last - first
    steps = polar // block // part[1]
    skip = part[0] * steps

    own_pieces = [(0, columns, raw)] if own else []
    swap_side, far_side = [
        [chunk for chunk in side if chunk[1] < last + 2 and chunk[2] > first - 2] for side in sides or ([], [])
    ]
    at = first // wide
    operands = list(own)
    specs = [
        pl.BlockSpec((2, rows, stop - start, block, azimuths), lambda t, odd, dest: (0, 0, 0, t + skip, 0))
        for start, stop, _ in own_pieces
    ]
    for side, place in ((swap_side, lambda odd: odd), (far_side, lambda odd: 1 - odd)):
        operands += [held for held, start, stop in side]
        specs += [
            pl.BlockSpec(
                (2, 2, stop - start, block, azimuths),
                lambda t, odd, dest, place=place: (0, place(odd[0]) * edge, 0, t + skip, 0),
            )
            for held, start, stop in side
        ]
    operands.append(table)
    specs.append(pl.BlockSpec((2, len(far_offsets), block, azimuths), lambda t, odd, dest: (0, 0, t + skip, 0)))
    out_spec = pl.BlockSpec((2, rows, wide, block, azimuths), lambda t, odd, dest: (0, 0, at, t + skip, 0))
    if partial is not None:
        operands.append(partial)
        specs.append(out_spec)
    aliases = {}
    if whole is not None:
        operands.append(whole)
        specs.append(pl.BlockSpec(memory_space=pl.ANY))
        aliases = {len(operands) + 1: 0}
    kind = jnp.bfloat16 if final else jnp.float32
    scratch = [
        pltpu.VMEM((3, rows + 4, wide + 4, block, LANES), jnp.float32),
        pltpu.VMEM((3, len(far_offsets), block, LANES), jnp.float32),
    ]
    if final:
        scratch.append(pltpu.VMEM((2, rows, wide, block, LANES), jnp.float32))
    swap_pieces, far_pieces = [[chunk[1:] for chunk in side] for side in (swap_side, far_side)]
    plan = (own_pieces, swap_pieces, far_pieces, first, last, columns, rows, partial is not None, final, whole is not None)
    share = ((2 / 3 if rows > 2 else 2 / 9) if own else 0) + ((1 / 3 if rows > 2 else 7 / 9) if sides else 0)
    return pl.pallas_call(
        functools.partial(translate_kernel, plan),
        grid_spec=pltpu.PrefetchScalarGridSpec(
            num_scalar_prefetch=2,
            grid=(steps,),
            in_specs=specs,
            out_specs=out_spec,
            scratch_shapes=scratch,
        ),
        out_shape=jax.ShapeDtypeStruct((2, rows, columns, polar, azimuths), kind),
        input_output_aliases=aliases,
        compiler_params=pltpu.CompilerParams(vmem_limit_bytes=VMEM_BYTES),
        cost_estimate=cost(22 * share * wide / columns / part[1] + 1),
    )(odd, dest, *operands)


def local(pattern, occupied, trans_fine, trans_coarse, theta_weights, phi_matrix, child_phase):
    _, count_rows, count_cols, polar, azimuths = pattern.shape
    groups = lax.axis_size("box")
    group = lax.axis_index("box")
    odd = (group % 2).astype(jnp.int32).reshape(1)
    partner = [(i, i ^ 1) for i in range(groups)]
    onward = [(i, i + 2) for i in range(0, groups - 2, 2)] + [(i, i - 2) for i in range(3, groups, 2)]
    chunks = 4
    width = count_cols // chunks
    starts = [k * width for k in range(chunks + 1)]

    flags = occupied.astype(jnp.bfloat16)[None, :, :, None, None]

    def chunk(values, k):
        return values[:, :, starts[k] : starts[k + 1]] * flags[:, :, starts[k] : starts[k + 1]]

    def flat(held):
        return held.reshape(2, count_rows, -1, azimuths)

    def placed(held, cols):
        ends = [sum(cols[: k + 1]) for k in range(len(cols))]
        return [(value, end - size, end) for value, size, end in zip(held, cols, ends)]

    def send(value, pairs):
        return lax.ppermute(value, "box", pairs)

    def onto(held, index, halos):
        return aggregate(held, width, halos, index, *fixed)

    parts = 2 if polar >= 32 else 1
    fine_plan = (trans_fine, occupied, odd)

    own = [chunk(pattern, 0)]
    rest, own[0] = lax.optimization_barrier((pattern, own[0]))
    edges = jnp.concatenate([rest[:, :, :, :2], rest[:, :, :, -2:]], axis=3) * flags
    own += [chunk(rest, k) for k in range(1, chunks)]

    swap0 = send(own[0], partner)
    own_halo = halo(edges).reshape(2, count_rows, -1, polar, azimuths)
    fine_sums = translate([rest], None, *fine_plan, 0, count_cols, final=False, raw=True, part=(0, parts))
    phases = (jnp.cos(child_phase), jnp.sin(child_phase))
    swap0, own_halo, fine_sums, phases, own, rest = lax.optimization_barrier(
        (swap0, own_halo, fine_sums, phases, own, rest)
    )
    inner, outer = bands(theta_weights, polar, width)
    fixed = (inner, outer, phi_matrix, *phases)

    swap1 = send(jnp.concatenate([own[1], own_halo], axis=2), partner)
    far0 = send(swap0, onward)
    coarse_own = aggregate([rest], count_cols, flat(own_halo), 0, *fixed, flags=occupied)
    swap0, swap1, far0, coarse_own, fine_sums, own, rest = lax.optimization_barrier(
        (swap0, swap1, far0, coarse_own, fine_sums, own, rest)
    )

    swap2 = send(own[2], partner)
    far1 = send(swap1, onward)
    swap_halo = flat(swap1[:, :, width:])
    if parts > 1:
        fine_sums = translate(
            [rest], None, *fine_plan, 0, count_cols, final=False, raw=True, whole=fine_sums, part=(1, parts)
        )
    coarse_swap = [onto([swap0, swap1], 0, swap_halo)]
    swap2, far0, far1, coarse_swap, fine_sums, own, swap_halo = lax.optimization_barrier(
        (swap2, far0, far1, coarse_swap, fine_sums, own, swap_halo)
    )

    swap3 = send(own[3], partner)
    far2 = send(swap2, onward)
    far_halo = flat(far1[:, :, width:])
    coarse_far = [onto([far0, far1], 0, far_halo)]
    coarse_swap.append(onto([swap2], 2, swap_halo))
    swap3, far2, far_halo, coarse_far, coarse_swap, fine_sums, swap_halo = lax.optimization_barrier(
        (swap3, far2, far_halo, coarse_far, coarse_swap, fine_sums, swap_halo)
    )

    far3 = send(swap3, onward)
    swap, far = [swap0, swap1, swap2, swap3], [far0, far1, far2]
    half = count_cols // 2
    coarse_swap.append(onto([swap3], 3, swap_halo))
    coarse_far.append(onto([far2], 2, far_halo))
    fine_sides = [placed(swap, [width] * 4), placed(far, [width] * 3)]
    local_fine = translate([], fine_sides, *fine_plan, 0, half, partial=fine_sums)
    far3, coarse_far, coarse_swap, local_fine, fine_sums = lax.optimization_barrier(
        (far3, coarse_far, coarse_swap, local_fine, fine_sums)
    )

    coarse_far.append(onto([far3], 3, far_halo))
    occupied_coarse = jnp.max(occupied.reshape(count_rows // 2, 2, count_cols // 2, 2), axis=(1, 3))
    coarse_sides = [placed(held, [width, width // 2, width // 2]) for held in (coarse_swap, coarse_far)]
    local_coarse = translate([coarse_own], coarse_sides, trans_coarse, occupied_coarse, odd, 0, half)
    fine_sides = [placed(swap, [width] * 4), placed([*far, far3], [width] * 4)]
    local_fine = translate([], fine_sides, *fine_plan, half, count_cols, partial=fine_sums, whole=local_fine)
    return local_fine, local_coarse


def solution(mesh):
    return jax.shard_map(
        local,
        mesh=mesh,
        in_specs=(
            P(None, "box", None, "dir", None),
            P("box", None),
            P(None, None, "dir", None),
            P(None, None, "dir", None),
            P("dir", None),
            P(),
            P(None, "dir", None),
        ),
        out_specs=(P(None, "box", None, "dir", None), P(None, "box", None, "dir", None)),
        check_vma=False,
    )
```

time: 478 us -> 140 us (0.29); the launches traced: 470 us -> 139 us
  other arithmetic: 430 us -> 7.74 us
  Pallas kernels: 0 us -> 83.5 us
  waiting for transfers between devices: 0.02 us -> 9.34 us
  starting transfers between devices: 20.1 us -> 26.4 us
    another operation x7 -> x1, other arithmetic: 230 us -> 0.01 us  [bands(): jnp.stack([jnp.pad(outer, ((0, 0), (4 * c, 4 * (group - 1 - c)))) for c i...]
    convert_element_type x13 -> x2, other arithmetic: 157 us -> 0.82 us  [the longest x1 0.68 us: local(): flags = occupied.astype(jnp.bfloat16)[None, :, :, None, None]]
    pallas_call x0 -> x12, Pallas kernels: none -> 83.5 us  [the longest x5 52.4 us: translate(): pl.pallas_call(functools.partial(translate_kernel, plan), grid_spec=pltpu...]
    mul x13 -> x3, other arithmetic: 24.4 us -> 3.78 us  [the longest x2 3.46 us: chunk(): values[:, :, starts[k]:starts[k + 1]] * flags[:, :, starts[k]:starts[k + 1]]]
    ppermute x6 -> x10, waiting for transfers between devices: 0.02 us -> 9.34 us  [the longest x8 9.34 us: send(): return lax.ppermute(value, 'box', pairs)]
    concatenate x2 -> x3, other arithmetic: 10.7 us -> 2.26 us  [the longest x1 1.28 us: halo(): return jnp.concatenate([before, after], axis=3)]
    reduce_sum x1 -> x0, other arithmetic: 7.68 us -> none  [aggregate(): real_part = jnp.sum(phase_cos * full[0] - phase_sin * full[1], axis=(1, 3))]
    ppermute x6 -> x10, starting transfers between devices: 20.1 us -> 26.4 us  [the longest x8 21.9 us: send(): return lax.ppermute(value, 'box', pairs)]
  transfers between devices with their start and end apart: 6 -> 10, of which waited for: 0 -> 4; matrix products, arithmetic and copies ran while one was open for 50% -> 5% of each run, Pallas kernels for 0% -> 36%
where the time goes in v1:
time: 140 us; the launch traced here: 139 us
  Pallas kernels  83.5 us (60%)
  starting transfers between devices  26.4 us (19%)
  local copies, waits for them, and re-layouts  11.3 us (8%)
  waiting for transfers between devices  9.34 us (7%)
  other arithmetic  7.74 us (6%)
    pallas_call x5, Pallas kernels, translate(): pl.pallas_call(functools.partial(translate_kernel, plan), grid_spec=pltpu...  52.4 us
    pallas_call x7, Pallas kernels, aggregate(): pl.pallas_call(functools.partial(aggregate_kernel, masked, group, pieces)...  31.1 us
    ppermute x8, starting transfers between devices, send(): return lax.ppermute(value, 'box', pairs)  21.9 us
    ppermute x8, waiting for transfers between devices, send(): return lax.ppermute(value, 'box', pairs)  9.34 us
    unnamed x48, local copies, waits for them, and re-layouts  5.27 us
    mul x2, other arithmetic, chunk(): values[:, :, starts[k]:starts[k + 1]] * flags[:, :, starts[k]:starts[k + 1]]  3.46 us
    ppermute x1, starting transfers between devices, halo(): before = lax.ppermute(masked[:, :, :, -2:], 'dir', up)  2.99 us
  transfers between devices with their start and end apart: 10, of which 4 were waited for; matrix products, arithmetic and copies ran while one was open for 5% of the time, Pallas kernels for 36%

profile of v1, /device:TPU:0, one launch (start us, length us, event | category | flops | bytes accessed | tf_op | source)
XLA Modules:
  0.0 139.4 jit_solution(11682349106192905600)
XLA Ops:
  0.6 0.7 convert_bitcast_fusion
  1.4 0.7 convert_element_type.10
  2.1 0.1 slice_bitcast_fusion
  2.1 2.1 %slice_multiply_fusion.3 = bf16[2,4,4,32,256]{4,3,2,1,0:T(8,128)(2,1)} fusion(bf16[2,4,16,32,256]{4,3,2,1,0:T(8,128)(2,1)} %refs_0_.3, bf16[4,4]{1,0:T(4,128)(2,1)S(1)} %get-tuple-element.108), kind=kLoop, calls=%fused_computation.4 | loop fusion | flops 262144 | bytes 1048608 | tf_op jit(solution)/shard_map/mul | solution.py:384
  4.3 1.5 %fusion = (bf16[2,4,16,2,256]{4,3,2,1,0:T(2,128)(2,1)S(1)}, bf16[2,4,16,2,256]{4,3,2,1,0:T(2,128)(2,1)S(1)}) fusion(bf16[2,4,16,32,256]{4,3,2,1,0:T(8,128)(2,1)} %refs_0_.3), kind=kLoop, calls=%fused_computation.34 | loop fusion | bytes 524288 | tf_op jit(solution)/shard_map/slice | solution.py:404
  5.8 0.3 maximum_multiply_fusion
  6.1 1.0 fusion.2
  7.0 3.0 %collective-permute-start.1 = (bf16[2,4,16,2,256]{4,3,2,1,0:T(2,128)(2,1)}, bf16[2,4,16,2,256]{4,3,2,1,0:T(2,128)(2,1)}, u32[]{:S(2)}, u32[]{:S(2)}) collective-permute-start(bf16[2,4,16,2,256]{4,3,2,1,0:T(2,128)(2,1)} %get-tuple-element.93), channel_id=1, source_target_pairs={{0,1},{1,2},{2,3},{4,5},{5,6},{6,7},{8,9},{9,10},{10,11},{12,13},{... | collective-permute-start | bytes 393224 | tf_op jit(solution)/shard_map/ppermute | solution.py:29
  10.0 1.4 %collective-permute-start.2 = (bf16[2,4,16,2,256]{4,3,2,1,0:T(2,128)(2,1)}, bf16[2,4,16,2,256]{4,3,2,1,0:T(2,128)(2,1)}, u32[]{:S(2)}, u32[]{:S(2)}) collective-permute-start(bf16[2,4,16,2,256]{4,3,2,1,0:T(2,128)(2,1)} %get-tuple-element.94), channel_id=1, source_target_pairs={{1,0},{2,1},{3,2},{5,4},{6,5},{7,6},{9,8},{10,9},{11,10},{13,12},{... | collective-permute-start | bytes 393224 | tf_op jit(solution)/shard_map/ppermute | solution.py:30
  11.5 2.4 %collective-permute-start = (bf16[2,4,4,32,256]{4,3,2,1,0:T(8,128)(2,1)}, bf16[2,4,4,32,256]{4,3,2,1,0:T(8,128)(2,1)}, u32[]{:S(2)}, u32[]{:S(2)}) collective-permute-start(bf16[2,4,4,32,256]{4,3,2,1,0:T(8,128)(2,1)} %slice_multiply_fusion.3), channel_id=1, source_target_pairs={{0,4},{4,0},{8,12},{12,8},{16,20},{20,16},{24,28},{28,24},{1,5},{5... | collective-permute-start | bytes 1572872 | tf_op jit(solution)/shard_map/ppermute | solution.py:394
  13.9 1.8 %fusion.1 = (f32[4,64,512]{2,1,0:T(8,128)S(1)}, f32[4,64,512]{2,1,0:T(8,128)S(1)}) fusion(f32[4,64,512]{2,1,0:T(8,128)S(1)} %copy-done.20), kind=kLoop, calls=%fused_computation.35 | loop fusion | bytes 1572864 | tf_op jit(solution)/shard_map/sin | solution.py:410
  15.7 1.3 slice_multiply_fusion
  17.1 0.0 copy-start.1
  17.1 1.3 copy-done.1
  18.4 7.4 %shard_map.86.refs_2_ = f32[2,4,16,32,256]{4,3,2,1,0:T(8,128)} custom-call(s32[1]{0:T(128)} %bitcast.odd_ref, s32[4,16]{1,0:T(4,128)S(1)} %copy-done.18, bf16[2,4,16,32,256]{4,3,2,1,0:T(8,128)(2,1)S(1)} %copy-done, bf16[2,40,32,256]{3,2,1,0:T(8,128)(2,1)S(1)} %copy-done.1), custom_call_target="tpu_custom_call" | custom-call | bytes 2749999 | tf_op jit(solution)/shard_map/pallas_call | solution.py:354
  25.8 0.0 collective-permute-done.1
  25.8 0.0 collective-permute-done.2
  25.8 1.3 pad_maximum_fusion.1
  27.1 0.2 copy.14
  27.3 0.0 collective-permute-done.refs_0_
  27.4 1.0 pad_maximum_fusion
  28.4 0.7 copy-done.14
  29.1 1.0 collective-permute-start.3
  30.0 0.1 add_convert_fusion
  30.2 0.1 slice.86.refs_3_.refs_2_
  30.3 4.3 %collective-permute-start.4 = (bf16[2,4,4,32,256]{4,3,2,1,0:T(8,128)(2,1)}, bf16[2,4,4,32,256]{4,3,2,1,0:T(8,128)(2,1)}, u32[]{:S(2)}, u32[]{:S(2)}) collective-permute-start(bf16[2,4,4,32,256]{4,3,2,1,0:T(8,128)(2,1)} %collective-permute-done.refs_0_), channel_id=1, source_target_pairs={{0,8},{8,16},{16,24},{12,4},{20,12},{28,20},{1,9},{9,17},{17,25},{... | collective-permute-start | bytes 1572872 | tf_op jit(solution)/shard_map/ppermute | solution.py:394
  34.6 0.1 fusion.3
  34.7 0.1 copy.17
  34.7 0.1 copy.18
  34.9 0.1 copy.19.refs_4_.refs_3_
  35.0 0.9 copy-done.15
  36.0 7.8 %shard_map.87.refs_0_ = bf16[2,2,8,64,512]{4,3,2,1,0:T(8,128)(2,1)S(1)} custom-call(s32[4,16]{1,0:T(4,128)S(1)} %copy-done.18, bf16[2,4,16,32,256]{4,3,2,1,0:T(8,128)(2,1)S(1)} %copy-done, bf16[2,4,64,256]{3,2,1,0:T(8,128)(2,1)S(1)} %bitcast.41, bf16[64,32]{1,0:T(8,128)(2,1)S(1)} %slice.86.refs_3_.refs_2_, bf16[4,64,16]{2,1,0:T(8,128)(2,1)S(1)} %copy.19.refs_4_.refs_3_, ...), custom_call_target="tpu_custom_call" | custom-call | bytes 2970000 | tf_op jit(solution)/shard_map/pallas_call | solution.py:121
  43.8 1.4 copy-done.7
  45.2 0.9 collective-permute-done.4.refs_0_.refs_3_
  46.0 3.4 %collective-permute-done.3.refs_1_.refs_0_ = bf16[2,4,6,32,256]{4,3,2,1,0:T(8,128)(2,1)} collective-permute-done((bf16[2,4,6,32,256]{4,3,2,1,0:T(8,128)(2,1)}, bf16[2,4,6,32,256]{4,3,2,1,0:T(8,128)(2,1)}, u32[]{:S(2)}, u32[]{:S(2)}) %collective-permute-start.3) | collective-permute-done | bytes 786464 | tf_op jit(solution)/shard_map/ppermute | solution.py:394
  49.5 3.5 %collective-permute-start.6 = (bf16[2,4,6,32,256]{4,3,2,1,0:T(8,128)(2,1)}, bf16[2,4,6,32,256]{4,3,2,1,0:T(8,128)(2,1)S(1)}, u32[]{:S(2)}, u32[]{:S(2)}) collective-permute-start(bf16[2,4,6,32,256]{4,3,2,1,0:T(8,128)(2,1)} %collective-permute-done.3.refs_1_.refs_0_), channel_id=1, source_target_pairs={{0,8},{8,16},{16,24},{12,4},{20,12},{28,20},{1,9},{9,17},{17,25},{... | collective-permute-start | bytes 2359304 | tf_op jit(solution)/shard_map/ppermute | solution.py:394
  53.0 0.1 collective-permute-start.5
  53.1 1.0 slice.82
  54.1 0.0 copy-start.2
  54.1 5.2 %shard_map.88.refs_1_ = bf16[2,2,4,64,512]{4,3,2,1,0:T(8,128)(2,1)S(1)} custom-call(bf16[2,4,4,32,256]{4,3,2,1,0:T(8,128)(2,1)} %collective-permute-done.refs_0_, bf16[2,4,6,32,256]{4,3,2,1,0:T(8,128)(2,1)} %collective-permute-done.3.refs_1_.refs_0_, bf16[2,4,64,256]{3,2,1,0:T(8,128)(2,1)S(1)} %bitcast.35, bf16[64,32]{1,0:T(8,128)(2,1)S(1)} %slice.86.refs_3_.refs_2_, ...), custom_call_target="tpu_custom_call" | custom-call | bytes 1650000 | tf_op jit(solution)/shard_map/pallas_call | solution.py:121
  59.3 0.0 copy-start.10
  59.3 0.0 copy-start.21
  59.3 7.4 %shard_map.89.refs_7_ = f32[2,4,16,32,256]{4,3,2,1,0:T(8,128)} custom-call(s32[1]{0:T(128)} %bitcast.odd_ref, s32[4,16]{1,0:T(4,128)S(1)} %copy-done.18, bf16[2,4,16,32,256]{4,3,2,1,0:T(8,128)(2,1)S(1)} %copy-done, bf16[2,40,32,256]{3,2,1,0:T(8,128)(2,1)S(1)} %copy-done.2, f32[2,4,16,32,256]{4,3,2,1,0:T(8,128)} %shard_map.86.refs_2_), custom_call_target="tpu_custom_call", output_to_operand_aliasing={{}: (4, {})} | custom-call | bytes 2749999 | tf_op jit(solution)/shard_map/pallas_call | solution.py:354
  66.8 0.0 collective-permute-done.5.refs_0_.refs_2_.refs_1_
  66.8 3.6 %collective-permute-done.6.refs_1_.refs_4_.refs_3_ = bf16[2,4,6,32,256]{4,3,2,1,0:T(8,128)(2,1)S(1)} collective-permute-done((bf16[2,4,6,32,256]{4,3,2,1,0:T(8,128)(2,1)}, bf16[2,4,6,32,256]{4,3,2,1,0:T(8,128)(2,1)S(1)}, u32[]{:S(2)}, u32[]{:S(2)}) %collective-permute-start.6) | collective-permute-done | bytes 786464 | tf_op jit(solution)/shard_map/ppermute | solution.py:394
  70.4 2.0 %collective-permute-start.7 = (bf16[2,4,4,32,256]{4,3,2,1,0:T(8,128)(2,1)S(1)}, bf16[2,4,4,32,256]{4,3,2,1,0:T(8,128)(2,1)}, u32[]{:S(2)}, u32[]{:S(2)}) collective-permute-start(bf16[2,4,4,32,256]{4,3,2,1,0:T(8,128)(2,1)S(1)} %copy-done.21), channel_id=1, source_target_pairs={{0,4},{4,0},{8,12},{12,8},{16,20},{20,16},{24,28},{28,24},{1,5},{5... | collective-permute-start | bytes 1572872 | tf_op jit(solution)/shard_map/ppermute | solution.py:394
  72.3 3.5 %collective-permute-start.8 = (bf16[2,4,4,32,256]{4,3,2,1,0:T(8,128)(2,1)S(1)}, bf16[2,4,4,32,256]{4,3,2,1,0:T(8,128)(2,1)S(1)}, u32[]{:S(2)}, u32[]{:S(2)}) collective-permute-start(bf16[2,4,4,32,256]{4,3,2,1,0:T(8,128)(2,1)S(1)} %collective-permute-done.5.refs_0_.refs_2_.refs_1_), channel_id=1, source_target_pairs={{0,8},{8,16},{16,24},{12,4},{20,12},{28,20},{1,9},{9,17},{17,25},{... | collective-permute-start | bytes 1572872 | tf_op jit(solution)/shard_map/ppermute | solution.py:394
  75.9 2.8 %shard_map.91.refs_2_ = bf16[2,2,2,64,512]{4,3,2,1,0:T(8,128)(2,1)S(1)} custom-call(bf16[2,4,4,32,256]{4,3,2,1,0:T(8,128)(2,1)S(1)} %collective-permute-done.5.refs_0_.refs_2_.refs_1_, bf16[2,4,64,256]{3,2,1,0:T(8,128)(2,1)S(1)} %bitcast.36, bf16[64,32]{1,0:T(8,128)(2,1)S(1)} %slice.86.refs_3_.refs_2_, bf16[4,64,16]{2,1,0:T(8,128)(2,1)S(1)} %copy.19.refs_4_.refs_3_, ...), custom_call_target="tpu_custom_call" | custom-call | bytes 990000 | tf_op jit(solution)/shard_map/pallas_call | solution.py:121
  78.7 0.9 copy-done.16
  79.5 5.1 %shard_map.90.refs_4_ = bf16[2,2,4,64,512]{4,3,2,1,0:T(8,128)(2,1)S(1)} custom-call(bf16[2,4,4,32,256]{4,3,2,1,0:T(8,128)(2,1)} %collective-permute-done.4.refs_0_.refs_3_, bf16[2,4,6,32,256]{4,3,2,1,0:T(8,128)(2,1)S(1)} %collective-permute-done.6.refs_1_.refs_4_.refs_3_, bf16[2,4,64,256]{3,2,1,0:T(8,128)(2,1)S(1)} %bitcast.38, ...), custom_call_target="tpu_custom_call" | custom-call | bytes 1650000 | tf_op jit(solution)/shard_map/pallas_call | solution.py:121
  84.6 0.0 collective-permute-done.7.refs_0_.refs_2_
  84.6 1.5 %collective-permute-done.8.refs_0_.refs_5_.refs_4_ = bf16[2,4,4,32,256]{4,3,2,1,0:T(8,128)(2,1)S(1)} collective-permute-done((bf16[2,4,4,32,256]{4,3,2,1,0:T(8,128)(2,1)S(1)}, bf16[2,4,4,32,256]{4,3,2,1,0:T(8,128)(2,1)S(1)}, u32[]{:S(2)}, u32[]{:S(2)}) %collective-permute-start.8) | collective-permute-done | bytes 524320 | tf_op jit(solution)/shard_map/ppermute | solution.py:394
  86.1 5.2 %collective-permute-start.9 = (bf16[2,4,4,32,256]{4,3,2,1,0:T(8,128)(2,1)}, bf16[2,4,4,32,256]{4,3,2,1,0:T(8,128)(2,1)}, u32[]{:S(2)}, u32[]{:S(2)}) collective-permute-start(bf16[2,4,4,32,256]{4,3,2,1,0:T(8,128)(2,1)} %collective-permute-done.7.refs_0_.refs_2_), channel_id=1, source_target_pairs={{0,8},{8,16},{16,24},{12,4},{20,12},{28,20},{1,9},{9,17},{17,25},{... | collective-permute-start | bytes 1572872 | tf_op jit(solution)/shard_map/ppermute | solution.py:394
  91.2 0.1 reshape.76
  91.3 0.1 reduce_max.9.dest_ref
  91.5 0.0 copy-start.3
  91.5 0.0 copy-start.6
  91.5 3.8 %shard_map.93.refs_3_ = bf16[2,2,2,64,512]{4,3,2,1,0:T(8,128)(2,1)S(1)} custom-call(bf16[2,4,4,32,256]{4,3,2,1,0:T(8,128)(2,1)} %collective-permute-done.7.refs_0_.refs_2_, bf16[2,4,64,256]{3,2,1,0:T(8,128)(2,1)S(1)} %bitcast.37, bf16[64,32]{1,0:T(8,128)(2,1)S(1)} %slice.86.refs_3_.refs_2_, bf16[4,64,16]{2,1,0:T(8,128)(2,1)S(1)} %copy.19.refs_4_.refs_3_, ...), custom_call_target="tpu_custom_call" | custom-call | bytes 990000 | tf_op jit(solution)/shard_map/pallas_call | solution.py:121
  95.3 2.8 %shard_map.92.refs_5_ = bf16[2,2,2,64,512]{4,3,2,1,0:T(8,128)(2,1)S(1)} custom-call(bf16[2,4,4,32,256]{4,3,2,1,0:T(8,128)(2,1)S(1)} %collective-permute-done.8.refs_0_.refs_5_.refs_4_, bf16[2,4,64,256]{3,2,1,0:T(8,128)(2,1)S(1)} %bitcast.39, bf16[64,32]{1,0:T(8,128)(2,1)S(1)} %slice.86.refs_3_.refs_2_, bf16[4,64,16]{2,1,0:T(8,128)(2,1)S(1)} %copy.19.refs_4_.refs_3_, ...), custom_call_target="tpu_custom_call" | custom-call | bytes 990000 | tf_op jit(solution)/shard_map/pallas_call | solution.py:121
  98.1 7.2 %shard_map.94.refs_8_ = bf16[2,4,16,32,256]{4,3,2,1,0:T(8,128)(2,1)} custom-call(s32[1]{0:T(128)} %bitcast.odd_ref, s32[4,16]{1,0:T(4,128)S(1)} %copy-done.18, bf16[2,4,4,32,256]{4,3,2,1,0:T(8,128)(2,1)} %collective-permute-done.refs_0_, bf16[2,4,6,32,256]{4,3,2,1,0:T(8,128)(2,1)} %collective-permute-done.3.refs_1_.refs_0_, ...), custom_call_target="tpu_custom_call" | custom-call | bytes 1539999 | tf_op jit(solution)/shard_map/pallas_call | solution.py:354
  105.3 3.6 %shard_map.96.refs_6_ = bf16[2,2,2,64,512]{4,3,2,1,0:T(8,128)(2,1)S(1)} custom-call(bf16[2,4,4,32,256]{4,3,2,1,0:T(8,128)(2,1)} %collective-permute-done.9.refs_5_.refs_0_, bf16[2,4,64,256]{3,2,1,0:T(8,128)(2,1)S(1)} %bitcast.40, bf16[64,32]{1,0:T(8,128)(2,1)S(1)} %slice.86.refs_3_.refs_2_, bf16[4,64,16]{2,1,0:T(8,128)(2,1)S(1)} %copy.19.refs_4_.refs_3_, ...), custom_call_target="tpu_custom_call" | custom-call | bytes 990000 | tf_op jit(solution)/shard_map/pallas_call | solution.py:121
  109.0 0.0 copy-start.11
  109.0 7.2 %shard_map.95 = bf16[2,4,16,32,256]{4,3,2,1,0:T(8,128)(2,1)} custom-call(s32[1]{0:T(128)} %bitcast.odd_ref, s32[4,16]{1,0:T(4,128)S(1)} %copy-done.18, bf16[2,4,6,32,256]{4,3,2,1,0:T(8,128)(2,1)} %collective-permute-done.3.refs_1_.refs_0_, bf16[2,4,4,32,256]{4,3,2,1,0:T(8,128)(2,1)S(1)} %copy-done.9, ...), custom_call_target="tpu_custom_call", output_to_operand_aliasing={{}: (10, {})} | custom-call | bytes 1539999 | tf_op jit(solution)/shard_map/pallas_call | solution.py:354
  116.2 23.1 %shard_map.97 = bf16[2,2,8,64,512]{4,3,2,1,0:T(8,128)(2,1)} custom-call(s32[1]{0:T(128)} %bitcast.odd_ref, s32[2,8]{1,0:T(2,128)S(1)} %reduce_max.9.dest_ref, bf16[2,2,8,64,512]{4,3,2,1,0:T(8,128)(2,1)} %copy-done.7, bf16[2,2,4,64,512]{4,3,2,1,0:T(8,128)(2,1)S(1)} %copy-done.11, bf16[2,2,2,64,512]{4,3,2,1,0:T(8,128)(2,1)S(1)} %copy-done.17, ...), custom_call_target="tpu_custom_call" | custom-call | bytes 7590000 | tf_op jit(solution)/shard_map/pallas_call | solution.py:354
  (45 shorter events, 0.2 us)
Async XLA Ops:
  0.6 13.2 %copy-start.20 = (f32[4,64,512]{2,1,0:T(8,128)S(1)}, f32[4,64,512]{2,1,0:T(8,128)}, u32[]{:S(2)}) copy-start(f32[4,64,512]{2,1,0:T(8,128)} %param.13) | copy-start | bytes 1572868
  2.1 13.6 %copy-start = (bf16[2,4,16,32,256]{4,3,2,1,0:T(8,128)(2,1)S(1)}, bf16[2,4,16,32,256]{4,3,2,1,0:T(8,128)(2,1)}, u32[]{:S(2)}) copy-start(bf16[2,4,16,32,256]{4,3,2,1,0:T(8,128)(2,1)} %refs_0_.3) | copy-start | bytes 6291460
  7.0 18.8 %collective-permute-start.1 = (bf16[2,4,16,2,256]{4,3,2,1,0:T(2,128)(2,1)}, bf16[2,4,16,2,256]{4,3,2,1,0:T(2,128)(2,1)}, u32[]{:S(2)}, u32[]{:S(2)}) collective-permute-start(bf16[2,4,16,2,256]{4,3,2,1,0:T(2,128)(2,1)} %get-tuple-element.93), channel_id=1, source_target_pairs={{0,1},{1,2},{2,3},{4,5},{5,6},{6,7},{8,9},{9,10},{10,11},{12,13},{... | collective-permute-start | bytes 393224 | tf_op jit(solution)/shard_map/ppermute | solution.py:29
  10.0 7.0 %copy-start.23 = (bf16[64,4]{0,1:T(4,128)(2,1)S(1)}, bf16[64,4]{0,1:T(4,128)(2,1)}, u32[]{:S(2)}) copy-start(bf16[64,4]{0,1:T(4,128)(2,1)} %param.11) | copy-start | bytes 1540
  10.0 7.0 %copy-start.18 = (s32[4,16]{1,0:T(4,128)S(1)}, s32[4,16]{1,0:T(4,128)}, u32[]{:S(2)}) copy-start(s32[4,16]{1,0:T(4,128)} %dest_ref.7) | copy-start | bytes 772
  10.0 15.8 %collective-permute-start.2 = (bf16[2,4,16,2,256]{4,3,2,1,0:T(2,128)(2,1)}, bf16[2,4,16,2,256]{4,3,2,1,0:T(2,128)(2,1)}, u32[]{:S(2)}, u32[]{:S(2)}) collective-permute-start(bf16[2,4,16,2,256]{4,3,2,1,0:T(2,128)(2,1)} %get-tuple-element.94), channel_id=1, source_target_pairs={{1,0},{2,1},{3,2},{5,4},{6,5},{7,6},{9,8},{10,9},{11,10},{13,12},{... | collective-permute-start | bytes 393224 | tf_op jit(solution)/shard_map/ppermute | solution.py:30
  11.5 15.9 %collective-permute-start = (bf16[2,4,4,32,256]{4,3,2,1,0:T(8,128)(2,1)}, bf16[2,4,4,32,256]{4,3,2,1,0:T(8,128)(2,1)}, u32[]{:S(2)}, u32[]{:S(2)}) collective-permute-start(bf16[2,4,4,32,256]{4,3,2,1,0:T(8,128)(2,1)} %slice_multiply_fusion.3), channel_id=1, source_target_pairs={{0,4},{4,0},{8,12},{12,8},{16,20},{20,16},{24,28},{28,24},{1,5},{5... | collective-permute-start | bytes 1572872 | tf_op jit(solution)/shard_map/ppermute | solution.py:394
  17.1 1.3 copy-start.1
  18.4 9.0 %copy-start.19 = (bf16[2,4,4,32,256]{4,3,2,1,0:T(8,128)(2,1)S(1)}, bf16[2,4,4,32,256]{4,3,2,1,0:T(8,128)(2,1)}, u32[]{:S(2)}) copy-start(bf16[2,4,4,32,256]{4,3,2,1,0:T(8,128)(2,1)} %get-tuple-element.47) | copy-start | bytes 1572868
  25.8 9.2 %copy-start.4 = (bf16[256,512]{1,0:T(8,128)(2,1)S(1)}, bf16[256,512]{1,0:T(8,128)(2,1)}, u32[]{:S(2)}) copy-start(bf16[256,512]{1,0:T(8,128)(2,1)} %refs_4_.7) | copy-start | bytes 786436
  28.4 0.7 copy-start.14
  29.1 20.4 %collective-permute-start.3 = (bf16[2,4,6,32,256]{4,3,2,1,0:T(8,128)(2,1)}, bf16[2,4,6,32,256]{4,3,2,1,0:T(8,128)(2,1)}, u32[]{:S(2)}, u32[]{:S(2)}) collective-permute-start(bf16[2,4,6,32,256]{4,3,2,1,0:T(8,128)(2,1)} %pad_maximum_fusion), channel_id=1, source_target_pairs={{0,4},{4,0},{8,12},{12,8},{16,20},{20,16},{24,28},{28,24},{1,5},{5... | collective-permute-start | bytes 2359304 | tf_op jit(solution)/shard_map/ppermute | solution.py:394
  30.3 15.8 %collective-permute-start.4 = (bf16[2,4,4,32,256]{4,3,2,1,0:T(8,128)(2,1)}, bf16[2,4,4,32,256]{4,3,2,1,0:T(8,128)(2,1)}, u32[]{:S(2)}, u32[]{:S(2)}) collective-permute-start(bf16[2,4,4,32,256]{4,3,2,1,0:T(8,128)(2,1)} %collective-permute-done.refs_0_), channel_id=1, source_target_pairs={{0,8},{8,16},{16,24},{12,4},{20,12},{28,20},{1,9},{9,17},{17,25},{... | collective-permute-start | bytes 1572872 | tf_op jit(solution)/shard_map/ppermute | solution.py:394
  35.0 1.0 copy-start.15
  36.0 17.0 %copy-start.22 = (bf16[2,4,4,32,256]{4,3,2,1,0:T(8,128)(2,1)S(1)}, bf16[2,4,4,32,256]{4,3,2,1,0:T(8,128)(2,1)}, u32[]{:S(2)}) copy-start(bf16[2,4,4,32,256]{4,3,2,1,0:T(8,128)(2,1)} %get-tuple-element.56) | copy-start | bytes 1572868
  43.8 1.4 copy-start.7
  49.5 20.9 %collective-permute-start.6 = (bf16[2,4,6,32,256]{4,3,2,1,0:T(8,128)(2,1)}, bf16[2,4,6,32,256]{4,3,2,1,0:T(8,128)(2,1)S(1)}, u32[]{:S(2)}, u32[]{:S(2)}) collective-permute-start(bf16[2,4,6,32,256]{4,3,2,1,0:T(8,128)(2,1)} %collective-permute-done.3.refs_1_.refs_0_), channel_id=1, source_target_pairs={{0,8},{8,16},{16,24},{12,4},{20,12},{28,20},{1,9},{9,17},{17,25},{... | collective-permute-start | bytes 2359304 | tf_op jit(solution)/shard_map/ppermute | solution.py:394
  53.0 13.8 %collective-permute-start.5 = (bf16[2,4,4,32,256]{4,3,2,1,0:T(8,128)(2,1)S(1)}, bf16[2,4,4,32,256]{4,3,2,1,0:T(8,128)(2,1)S(1)}, u32[]{:S(2)}, u32[]{:S(2)}) collective-permute-start(bf16[2,4,4,32,256]{4,3,2,1,0:T(8,128)(2,1)S(1)} %copy-done.22), channel_id=1, source_target_pairs={{0,4},{4,0},{8,12},{12,8},{16,20},{20,16},{24,28},{28,24},{1,5},{5... | collective-permute-start | bytes 1572872 | tf_op jit(solution)/shard_map/ppermute | solution.py:394
  54.1 21.8 %copy-start.12 = (bf16[2,4,2,32,256]{4,3,2,1,0:T(8,128)(2,1)}, bf16[2,4,2,32,256]{4,3,2,1,0:T(8,128)(2,1)S(1)}, u32[]{:S(2)}) copy-start(bf16[2,4,2,32,256]{4,3,2,1,0:T(8,128)(2,1)S(1)} %slice.82) | copy-start | bytes 786436
  54.1 5.2 %copy-start.2 = (bf16[2,40,32,256]{3,2,1,0:T(8,128)(2,1)S(1)}, bf16[2,40,32,256]{3,2,1,0:T(8,128)(2,1)}, u32[]{:S(2)}) copy-start(bf16[2,40,32,256]{3,2,1,0:T(8,128)(2,1)} %refs_6_.3) | copy-start | bytes 3932164
  59.3 7.5 %copy-start.10 = (bf16[2,2,4,64,512]{4,3,2,1,0:T(8,128)(2,1)}, bf16[2,2,4,64,512]{4,3,2,1,0:T(8,128)(2,1)S(1)}, u32[]{:S(2)}) copy-start(bf16[2,2,4,64,512]{4,3,2,1,0:T(8,128)(2,1)S(1)} %shard_map.88.refs_1_) | copy-start | bytes 3145732
  59.3 11.0 %copy-start.21 = (bf16[2,4,4,32,256]{4,3,2,1,0:T(8,128)(2,1)S(1)}, bf16[2,4,4,32,256]{4,3,2,1,0:T(8,128)(2,1)}, u32[]{:S(2)}) copy-start(bf16[2,4,4,32,256]{4,3,2,1,0:T(8,128)(2,1)} %get-tuple-element.63) | copy-start | bytes 1572868
  66.8 17.8 %copy-start.8 = (bf16[2,4,4,32,256]{4,3,2,1,0:T(8,128)(2,1)}, bf16[2,4,4,32,256]{4,3,2,1,0:T(8,128)(2,1)S(1)}, u32[]{:S(2)}) copy-start(bf16[2,4,4,32,256]{4,3,2,1,0:T(8,128)(2,1)S(1)} %collective-permute-done.5.refs_0_.refs_2_.refs_1_) | copy-start | bytes 1572868
  70.4 14.2 %copy-start.5 = (bf16[2,4,6,32,256]{4,3,2,1,0:T(8,128)(2,1)}, bf16[2,4,6,32,256]{4,3,2,1,0:T(8,128)(2,1)S(1)}, u32[]{:S(2)}) copy-start(bf16[2,4,6,32,256]{4,3,2,1,0:T(8,128)(2,1)S(1)} %collective-permute-done.6.refs_1_.refs_4_.refs_3_) | copy-start | bytes 2359300
  70.4 14.2 %collective-permute-start.7 = (bf16[2,4,4,32,256]{4,3,2,1,0:T(8,128)(2,1)S(1)}, bf16[2,4,4,32,256]{4,3,2,1,0:T(8,128)(2,1)}, u32[]{:S(2)}, u32[]{:S(2)}) collective-permute-start(bf16[2,4,4,32,256]{4,3,2,1,0:T(8,128)(2,1)S(1)} %copy-done.21), channel_id=1, source_target_pairs={{0,4},{4,0},{8,12},{12,8},{16,20},{20,16},{24,28},{28,24},{1,5},{5... | collective-permute-start | bytes 1572872 | tf_op jit(solution)/shard_map/ppermute | solution.py:394
  72.3 13.7 %collective-permute-start.8 = (bf16[2,4,4,32,256]{4,3,2,1,0:T(8,128)(2,1)S(1)}, bf16[2,4,4,32,256]{4,3,2,1,0:T(8,128)(2,1)S(1)}, u32[]{:S(2)}, u32[]{:S(2)}) collective-permute-start(bf16[2,4,4,32,256]{4,3,2,1,0:T(8,128)(2,1)S(1)} %collective-permute-done.5.refs_0_.refs_2_.refs_1_), channel_id=1, source_target_pairs={{0,8},{8,16},{16,24},{12,4},{20,12},{28,20},{1,9},{9,17},{17,25},{... | collective-permute-start | bytes 1572872 | tf_op jit(solution)/shard_map/ppermute | solution.py:394
  78.6 0.9 copy-start.16
  79.5 11.9 %copy-start.13 = (bf16[2,4,2,32,256]{4,3,2,1,0:T(8,128)(2,1)S(1)}, bf16[2,4,2,32,256]{4,3,2,1,0:T(8,128)(2,1)}, u32[]{:S(2)}) copy-start(bf16[2,4,2,32,256]{4,3,2,1,0:T(8,128)(2,1)} %copy-done.12) | copy-start | bytes 786436
  86.1 19.3 %collective-permute-start.9 = (bf16[2,4,4,32,256]{4,3,2,1,0:T(8,128)(2,1)}, bf16[2,4,4,32,256]{4,3,2,1,0:T(8,128)(2,1)}, u32[]{:S(2)}, u32[]{:S(2)}) collective-permute-start(bf16[2,4,4,32,256]{4,3,2,1,0:T(8,128)(2,1)} %collective-permute-done.7.refs_0_.refs_2_), channel_id=1, source_target_pairs={{0,8},{8,16},{16,24},{12,4},{20,12},{28,20},{1,9},{9,17},{17,25},{... | collective-permute-start | bytes 1572872 | tf_op jit(solution)/shard_map/ppermute | solution.py:394
  91.5 6.6 %copy-start.3 = (bf16[2,40,32,256]{3,2,1,0:T(8,128)(2,1)S(1)}, bf16[2,40,32,256]{3,2,1,0:T(8,128)(2,1)}, u32[]{:S(2)}) copy-start(bf16[2,40,32,256]{3,2,1,0:T(8,128)(2,1)} %refs_6_.3) | copy-start | bytes 3932164
  91.5 6.6 %copy-start.6 = (bf16[2,4,6,32,256]{4,3,2,1,0:T(8,128)(2,1)S(1)}, bf16[2,4,6,32,256]{4,3,2,1,0:T(8,128)(2,1)}, u32[]{:S(2)}) copy-start(bf16[2,4,6,32,256]{4,3,2,1,0:T(8,128)(2,1)} %copy-done.5) | copy-start | bytes 2359300
  91.5 6.6 %copy-start.9 = (bf16[2,4,4,32,256]{4,3,2,1,0:T(8,128)(2,1)S(1)}, bf16[2,4,4,32,256]{4,3,2,1,0:T(8,128)(2,1)}, u32[]{:S(2)}) copy-start(bf16[2,4,4,32,256]{4,3,2,1,0:T(8,128)(2,1)} %copy-done.8) | copy-start | bytes 1572868
  109.0 7.3 %copy-start.11 = (bf16[2,2,4,64,512]{4,3,2,1,0:T(8,128)(2,1)S(1)}, bf16[2,2,4,64,512]{4,3,2,1,0:T(8,128)(2,1)}, u32[]{:S(2)}) copy-start(bf16[2,2,4,64,512]{4,3,2,1,0:T(8,128)(2,1)} %copy-done.10) | copy-start | bytes 3145732
  109.0 7.2 %copy-start.17 = (bf16[2,2,2,64,512]{4,3,2,1,0:T(8,128)(2,1)S(1)}, bf16[2,2,2,64,512]{4,3,2,1,0:T(8,128)(2,1)}, u32[]{:S(2)}) copy-start(bf16[2,2,2,64,512]{4,3,2,1,0:T(8,128)(2,1)} %copy-done.16) | copy-start | bytes 1572868
